TPU v7x, 32 devices: a whole 2x2x4 slice. The times are simulated.
32 devices in a mesh: lift: 4 (over z), tile: 8 (over y, x, core).
Axes of the slice: x: 2, y: 2, z: 4, core: 2. Of those that a mesh axis runs over, the one named last changes fastest.
Arguments:
- oxygen: float32 [4, 16, 8, 256, 256], P('lift', None, 'tile'), may hold values from 0 to 1
- velocity: float32 [4, 16, 8, 256, 256], P('lift', None, 'tile'), may hold values from 0.2 to 1
- spacing: float32 [4], P('lift'), may hold values from 1 to 2
- inlets: int32 [4, 8, 256, 256], P('lift', 'tile'), may hold values 0 or 1
- proj_x: float32 [4, 8, 4, 256, 256], P('lift', 'tile'), may hold values from -1 to 1
- proj_y: float32 [4, 8, 4, 256, 256], P('lift', 'tile'), may hold values from -1 to 1
- sources: int32 [4, 8, 4], P('lift', 'tile'), may hold values from 0 to 7, as said below
Outputs:
- oxygen_next: float32 [4, 16, 8, 256, 256], P('lift', None, 'tile')
Inputs may be any that keep to these rules, and one draw needn't show every extreme that they name: sources[l, t, 0] is the tile (t + 4) % 8; the other entries may be any tile of the lift below; entries of lift 0 are not used.
All inputs are finite; a program needn't handle non-finite values. No bound on the sum of `inlets` on one device may be relied on, other than what follows from the above.
Results may differ from a plain program's by a relative error of at most 0.0001.
Values sent between devices are 32-bit elements; how exact they have to be, the bound alone decides.
A program may use at most 128 MiB of HBM per device.

v0:
```python
import jax
import jax.numpy as jnp
from jax import lax
from jax.sharding import PartitionSpec as P

TCOL = 4
STEPS = 2


TIME_STEP = 0.1
INJECT_RATE = 2.0
AMBIENT = 1.0
HIGHEST = lax.Precision.HIGHEST


def shifted(value, axis, steps):
    count = lax.axis_size(axis)
    initial, last = (max(0, -steps), min(count, count - steps))
    return lax.ppermute(value, axis, [(source, source + steps) for source in range(initial, last)])


def on_device(oxygen, velocity, spacing, inlets, proj_x, proj_y, sources):
    field = oxygen[0, :, 0]
    speed = velocity[0, :, 0]
    inverse = 1.0 / (spacing[0] * spacing[0])
    inject = INJECT_RATE * inlets[0, 0].astype(jnp.float32)
    blocks_x = proj_x[0, 0]
    blocks_y = proj_y[0, 0]
    listed = sources[0, 0]
    tile_count = lax.axis_size("tile")
    tile_index = lax.axis_index("tile")
    lift_index = lax.axis_index("lift")
    is_top = lift_index == lax.axis_size("lift") - 1
    column = tile_index % TCOL
    onehot = (listed[:, None] == jnp.arange(tile_count, dtype=jnp.int32)[None, :]).astype(
        jnp.float32
    )
    depth = field.shape[0]
    for step_index in range(STEPS):
        rims = [
            (TCOL, field[:, -1, :]),
            (-TCOL, field[:, 0, :]),
            (1, field[:, :, -1]),
            (-1, field[:, :, 0]),
        ]
        arrived = []
        for offset, rim in rims:
            arrived.append(shifted(rim, "tile", offset))
        low_y = jnp.where(column == 0, 0.0, arrived[2])
        high_y = jnp.where(column == TCOL - 1, 0.0, arrived[3])
        beside_x = jnp.concatenate([arrived[0][:, None, :], field, arrived[1][:, None, :]], axis=1)
        beside_y = jnp.concatenate([low_y[:, :, None], field, high_y[:, :, None]], axis=2)
        beside_all = (
            beside_x[:, 2:, :] + beside_x[:, :-2, :] + beside_y[:, :, 2:] + beside_y[:, :, :-2]
        )
        lapl = (beside_all - 4.0 * field) * inverse
        top_plane = field[depth - 1]
        bottom_plane = field[0]
        pieces = jnp.einsum("kba,bc,kcd->kad", blocks_x, bottom_plane, blocks_y, precision=HIGHEST)
        outgoing = jnp.einsum("ks,kad->sad", onehot, pieces, precision=HIGHEST)
        whole_tops = lax.all_gather(top_plane[None], "tile", axis=0, tiled=True)
        tops_below = shifted(whole_tops, "lift", 1)
        terms_above = shifted(outgoing, "lift", -1)
        summed = lax.psum_scatter(terms_above, "tile", scatter_dimension=0, tiled=True)[0]
        picked = jnp.take(tops_below, listed, axis=0)
        ghost_below = jnp.einsum("kab,kbc,kdc->ad", blocks_x, picked, blocks_y, precision=HIGHEST)
        ghost_above = jnp.where(is_top, AMBIENT, summed)
        stacked = jnp.concatenate([ghost_below[None], field, ghost_above[None]], axis=0)
        under = stacked[:-2]
        over = stacked[2:]
        change = lapl + over + under - 2.0 * field - speed * (field - under)
        change = change.at[0].add(inject * (1.0 - field[0]))
        field = field + TIME_STEP * change
    return field[None, :, None]


def solution(mesh):
    return jax.shard_map(
        on_device,
        mesh=mesh,
        in_specs=(
            P("lift", None, "tile", None, None),
            P("lift", None, "tile", None, None),
            P("lift"),
            P("lift", "tile", None, None),
            P("lift", "tile", None, None, None),
            P("lift", "tile", None, None, None),
            P("lift", "tile", None),
        ),
        out_specs=P("lift", None, "tile", None, None),
        check_vma=False,
    )
```

profile of v0, /device:TPU:0, one launch (start us, length us, event | category | flops | bytes accessed | tf_op | source)
XLA Modules:
  0.0 270.5 jit_solution(10375125407427766381)
XLA Ops:
  8.5 2.8 %fusion.34 = f32[256,4,256]{0,2,1:T(8,128)S(1)} fusion(f32[1,1,4,256,256]{4,3,2,1,0:T(8,128)S(1)} %copy-done, f32[1,16,1,256,256]{4,3,2,1,0:T(8,128)} %param.13), kind=kOutput, calls=%fused_computation.56 | convolution fusion | flops 805306368 | bytes 2359296 | tf_op jit(solution)/shard_map/kba,bc,kcd->kad/dot_general | solution.py:59
  12.5 3.2 %fusion.38 = f32[8,256,256]{2,0,1:T(8,128)} fusion(f32[4,256,256]{2,1,0:T(8,128)S(1)} %fusion.26, s32[4]{0:T(128)S(1)} %bitcast.95), kind=kOutput, calls=%fused_computation.60 | convolution fusion | flops 25165856 | bytes 3145744 | tf_op jit(solution)/shard_map/ks,kad->sad/dot_general | solution.py:60
  15.7 2.9 %copy.131 = f32[8,256,256]{1,2,0:T(8,128)} copy(f32[8,256,256]{2,0,1:T(8,128)} %fusion.38) | data formatting | bytes 4194304 | tf_op jit(solution)/shard_map/ks,kad->sad/dot_general | solution.py:60
  19.9 49.6 %collective-permute-done.4 = f32[8,256,256]{1,2,0:T(8,128)} collective-permute-done((f32[8,256,256]{1,2,0:T(8,128)}, f32[8,256,256]{1,2,0:T(8,128)}, u32[]{:S(2)}, u32[]{:S(2)}) %collective-permute-start.4) | collective-permute-done | bytes 2097184 | tf_op jit(solution)/shard_map/ppermute | solution.py:19
  69.6 5.0 %collective-permute-start.5 = (f32[8,256,256]{2,1,0:T(8,128)}, f32[8,256,256]{2,1,0:T(8,128)}, u32[]{:S(2)}, u32[]{:S(2)}) collective-permute-start(f32[8,256,256]{2,1,0:T(8,128)} %bitcast.97), channel_id=1, source_target_pairs={{0,8},{8,16},{16,24},{1,9},{9,17},{17,25},{2,10},{10,18},{18,26},{... | collective-permute-start | bytes 6291464 | tf_op jit(solution)/shard_map/ppermute | solution.py:19
  74.6 5.1 %fusion.61 = (f32[16,256,1]{2,1,0:T(8,128)}, f32[16,256,1]{2,1,0:T(8,128)}) fusion(f32[16,256,256]{2,1,0:T(8,128)} %bitcast.86), kind=kLoop, calls=%fused_computation.98 | loop fusion | bytes 65536 | tf_op jit(solution)/shard_map/slice | solution.py:44
  79.7 2.3 copy.162
  83.3 2.2 copy.163
  85.5 3.0 %collective-permute-start.3 = (f32[16,256]{1,0:T(8,128)S(1)}, f32[16,256]{1,0:T(8,128)S(1)}, u32[]{:S(2)}, u32[]{:S(2)}) collective-permute-start(f32[16,256]{1,0:T(8,128)S(1)} %bitcast.90), channel_id=1, source_target_pairs={{0,1},{1,2},{2,3},{3,4},{4,5},{5,6},{6,7},{8,9},{9,10},{10,11},{11... | collective-permute-start | bytes 49160 | tf_op jit(solution)/shard_map/ppermute | solution.py:19
  88.5 5.4 %copy.121 = f32[1,16,1,256,256]{3,4,1,2,0:T(8,128)} copy(f32[1,16,1,256,256]{4,3,2,1,0:T(8,128)} %param.13) | data formatting | bytes 8388608 | tf_op args[0]
  93.9 3.9 %slice_reduce_fusion.3 = (f32[16,256]{1,0:T(8,128)S(1)}, f32[16,256]{1,0:T(8,128)S(1)}) fusion(f32[16,256,256]{1,2,0:T(8,128)} %bitcast.84), kind=kLoop, calls=%fused_computation.41 | loop fusion | bytes 65536 | tf_op jit(solution)/shard_map/slice | solution.py:42
  99.1 4.7 %collective-permute-start.1 = (f32[16,256]{1,0:T(8,128)S(1)}, f32[16,256]{1,0:T(8,128)S(1)}, u32[]{:S(2)}, u32[]{:S(2)}) collective-permute-start(f32[16,256]{1,0:T(8,128)S(1)} %get-tuple-element.33), channel_id=1, source_target_pairs={{0,4},{1,5},{2,6},{3,7},{8,12},{9,13},{10,14},{11,15},{16,20},{17,... | collective-permute-start | bytes 49160 | tf_op jit(solution)/shard_map/ppermute | solution.py:19
  103.9 5.4 %copy.135 = f32[1,16,1,256,256]{3,4,1,2,0:T(8,128)} copy(f32[1,16,1,256,256]{4,3,2,1,0:T(8,128)} %param.14) | data formatting | bytes 8388608 | tf_op args[1]
  117.6 3.2 %gather_fusion = f32[4,256,256]{2,1,0:T(8,128)} fusion(f32[8,256,256]{2,1,0:T(8,128)} %collective-permute-done.5, s32[1024]{0:T(1024)S(1)} %pad_clamp_fusion), kind=kCustom, calls=%fused_computation.clone | custom fusion | bytes 2097168 | tf_op jit(solution)/shard_map/jit(_take)/gather | solution.py:65
  120.7 2.7 fusion.32
  124.5 7.6 %fusion.14 = f32[16,256,256]{1,2,0:T(8,128)S(1)} fusion(f32[16,256,256]{1,2,0:T(8,128)S(1)} %bitcast.85, f32[1,256,256]{1,2,0:T(8,128)S(1)} %convolution_bitcast_fusion.1, f32[1,256,256]{1,2,0:T(8,128)S(1)} %broadcast_select_fusion.1, f32[16,256,1]{1,2,0:T(1,128)S(1)} %copy.127, f32[16,256,1]{1,2,0:T(1,128)S(1)} %copy.125, f32[16,1,256]{1,2,0:T(8,128)} %copy.123, ...), kind=kLoop, calls=%fused_computation.23 | loop fusion | flops 19922944 | bytes 13172740 | tf_op jit(solution)/shard_map/sub | solution.py:71
  136.7 2.8 %fusion.30 = f32[256,4,256]{0,2,1:T(8,128)S(1)} fusion(f32[1,1,4,256,256]{4,3,2,1,0:T(8,128)S(1)} %copy-done, f32[16,256,256]{1,2,0:T(8,128)} %copy-done.1), kind=kOutput, calls=%fused_computation.52 | convolution fusion | flops 805306368 | bytes 2359296 | tf_op jit(solution)/shard_map/kba,bc,kcd->kad/dot_general | solution.py:59
  140.6 3.3 %fusion.36 = f32[8,256,256]{2,0,1:T(8,128)} fusion(f32[4,256,256]{2,1,0:T(8,128)S(1)} %fusion.23, s32[4]{0:T(128)S(1)} %bitcast.96), kind=kOutput, calls=%fused_computation.58 | convolution fusion | flops 25165856 | bytes 3145744 | tf_op jit(solution)/shard_map/ks,kad->sad/dot_general | solution.py:60
  143.9 3.0 %copy.144 = f32[8,256,256]{1,2,0:T(8,128)} copy(f32[8,256,256]{2,0,1:T(8,128)} %fusion.36) | data formatting | bytes 4194304 | tf_op jit(solution)/shard_map/ks,kad->sad/dot_general | solution.py:60
  148.1 47.6 %collective-permute-done.10 = f32[8,256,256]{1,2,0:T(8,128)} collective-permute-done((f32[8,256,256]{1,2,0:T(8,128)}, f32[8,256,256]{1,2,0:T(8,128)}, u32[]{:S(2)}, u32[]{:S(2)}) %collective-permute-start.10) | collective-permute-done | bytes 2097184 | tf_op jit(solution)/shard_map/ppermute | solution.py:19
  195.8 4.6 %collective-permute-start.11 = (f32[8,256,256]{2,1,0:T(8,128)}, f32[8,256,256]{2,1,0:T(8,128)}, u32[]{:S(2)}, u32[]{:S(2)}) collective-permute-start(f32[8,256,256]{2,1,0:T(8,128)} %all-gather.4.cloned.1.call-done), channel_id=1, source_target_pairs={{0,8},{8,16},{16,24},{1,9},{9,17},{17,25},{2,10},{10,18},{18,26},{... | collective-permute-start | bytes 6291464 | tf_op jit(solution)/shard_map/ppermute | solution.py:19
  203.0 4.2 %slice_reduce_fusion.1 = (f32[16,256]{1,0:T(8,128)S(1)}, f32[16,256]{1,0:T(8,128)S(1)}) fusion(f32[16,256,256]{1,2,0:T(8,128)} %copy-done.1), kind=kLoop, calls=%fused_computation.39 | loop fusion | bytes 65536 | tf_op jit(solution)/shard_map/slice | solution.py:42
  208.4 4.5 %collective-permute-start.7 = (f32[16,256]{1,0:T(8,128)S(1)}, f32[16,256]{1,0:T(8,128)S(1)}, u32[]{:S(2)}, u32[]{:S(2)}) collective-permute-start(f32[16,256]{1,0:T(8,128)S(1)} %get-tuple-element.31), channel_id=1, source_target_pairs={{0,4},{1,5},{2,6},{3,7},{8,12},{9,13},{10,14},{11,15},{16,20},{17,... | collective-permute-start | bytes 49160 | tf_op jit(solution)/shard_map/ppermute | solution.py:19
  214.3 2.0 copy.137
  216.4 2.0 copy.138
  218.5 18.7 %reduce-scatter.5.cloned.1.call-done = f32[1,256,256]{1,2,0:T(8,128)} async-done(((f32[8,256,256]{1,2,0:T(8,128)}), f32[1,256,256]{1,2,0:T(8,128)}) %reduce-scatter.5.cloned.1.call-update) | async-done | bytes 262160 | tf_op jit(solution)/shard_map/reduce_scatter | solution.py:64
  238.1 3.3 %collective-permute-done.11 = f32[8,256,256]{2,1,0:T(8,128)} collective-permute-done((f32[8,256,256]{2,1,0:T(8,128)}, f32[8,256,256]{2,1,0:T(8,128)}, u32[]{:S(2)}, u32[]{:S(2)}) %collective-permute-start.11) | collective-permute-done | bytes 2097184 | tf_op jit(solution)/shard_map/ppermute | solution.py:19
  241.5 3.2 %gather_fusion.1 = f32[4,256,256]{2,1,0:T(8,128)} fusion(f32[8,256,256]{2,1,0:T(8,128)} %collective-permute-done.11, s32[1024]{0:T(1024)S(1)} %pad_clamp_fusion), kind=kCustom, calls=%fused_computation.1.clone | custom fusion | bytes 2097168 | tf_op jit(solution)/shard_map/jit(_take)/gather | solution.py:65
  244.6 2.7 fusion.28
  248.4 7.6 %fusion.3 = f32[16,256,256]{1,2,0:T(8,128)S(1)} fusion(f32[16,256,256]{1,2,0:T(8,128)S(1)} %copy-done.2, f32[1,256,256]{1,2,0:T(8,128)S(1)} %convolution_bitcast_fusion, f32[1,256,256]{1,2,0:T(8,128)S(1)} %broadcast_select_fusion, f32[16,256,1]{1,2,0:T(1,128)S(1)} %broadcast_in_dim.70, f32[16,256,1]{1,2,0:T(1,128)S(1)} %copy.140, f32[16,1,256]{1,2,0:T(8,128)} %copy.138, ...), kind=kLoop, calls=%fused_computation.6 | loop fusion | flops 19922944 | bytes 13172740 | tf_op jit(solution)/shard_map/sub | solution.py:71
  256.1 2.5 add_bitcast_fusion
  258.6 5.3 %copy.149 = f32[1,16,1,256,256]{4,3,2,1,0:T(8,128)} copy(f32[1,16,1,256,256]{3,4,1,2,0:T(8,128)} %add_bitcast_fusion) | data formatting | bytes 8388608 | tf_op jit(solution)/shard_map/broadcast_in_dim | solution.py:74
  (71 shorter events, 29.8 us)
Async XLA Ops:
  6.5 2.0 copy-start
  6.5 4.8 %copy-start.4 = (f32[1,1,4,256,256]{4,3,2,1,0:T(8,128)S(1)}, f32[1,1,4,256,256]{4,3,2,1,0:T(8,128)}, u32[]{:S(2)}) copy-start(f32[1,1,4,256,256]{4,3,2,1,0:T(8,128)} %param.18) | copy-start | bytes 3145732
  6.5 5.9 %copy-start.6 = (s32[1,1,4]{2,1,0:T(1,128)S(1)}, s32[1,1,4]{2,1,0:T(1,128)}, u32[]{:S(2)}) copy-start(s32[1,1,4]{2,1,0:T(1,128)} %param.19) | copy-start | bytes 52
  6.5 63.1 %all-gather.6.cloned.1.call-start = ((), (), s32[]{:S(2)}) async-start(), calls=%async_computation.5 | async-start | bytes 2359296 | tf_op jit(solution)/shard_map/all_gather | solution.py:61
  8.5 106.7 %reduce-scatter.3.cloned.1.call-start = ((), (), s32[]{:S(2)}) async-start(), calls=%async_computation.2 | async-start | bytes 2359296 | tf_op jit(solution)/shard_map/reduce_scatter | solution.py:64
  18.6 50.9 %collective-permute-start.4 = (f32[8,256,256]{1,2,0:T(8,128)}, f32[8,256,256]{1,2,0:T(8,128)}, u32[]{:S(2)}, u32[]{:S(2)}) collective-permute-start(f32[8,256,256]{1,2,0:T(8,128)} %copy.131), channel_id=1, source_target_pairs={{8,0},{16,8},{24,16},{9,1},{17,9},{25,17},{10,2},{18,10},{26,18},{... | collective-permute-start | bytes 6291464 | tf_op jit(solution)/shard_map/ppermute | solution.py:19
  69.5 126.3 %all-gather.4.cloned.1.call-start = ((), (), s32[]{:S(2)}) async-start(), calls=%async_computation.4 | async-start | bytes 2359296 | tf_op jit(solution)/shard_map/all_gather | solution.py:61
  69.6 48.0 %collective-permute-start.5 = (f32[8,256,256]{2,1,0:T(8,128)}, f32[8,256,256]{2,1,0:T(8,128)}, u32[]{:S(2)}, u32[]{:S(2)}) collective-permute-start(f32[8,256,256]{2,1,0:T(8,128)} %bitcast.97), channel_id=1, source_target_pairs={{0,8},{8,16},{16,24},{1,9},{9,17},{17,25},{2,10},{10,18},{18,26},{... | collective-permute-start | bytes 6291464 | tf_op jit(solution)/shard_map/ppermute | solution.py:19
  82.0 29.1 %collective-permute-start.2 = (f32[16,256]{1,0:T(8,128)S(1)}, f32[16,256]{1,0:T(8,128)S(1)}, u32[]{:S(2)}, u32[]{:S(2)}) collective-permute-start(f32[16,256]{1,0:T(8,128)S(1)} %bitcast.89), channel_id=1, source_target_pairs={{1,0},{2,1},{3,2},{4,3},{5,4},{6,5},{7,6},{9,8},{10,9},{11,10},{12... | collective-permute-start | bytes 49160 | tf_op jit(solution)/shard_map/ppermute | solution.py:19
  85.5 25.6 %collective-permute-start.3 = (f32[16,256]{1,0:T(8,128)S(1)}, f32[16,256]{1,0:T(8,128)S(1)}, u32[]{:S(2)}, u32[]{:S(2)}) collective-permute-start(f32[16,256]{1,0:T(8,128)S(1)} %bitcast.90), channel_id=1, source_target_pairs={{0,1},{1,2},{2,3},{3,4},{4,5},{5,6},{6,7},{8,9},{9,10},{10,11},{11... | collective-permute-start | bytes 49160 | tf_op jit(solution)/shard_map/ppermute | solution.py:19
  97.8 13.3 %collective-permute-start = (f32[16,256]{1,0:T(8,128)S(1)}, f32[16,256]{1,0:T(8,128)S(1)}, u32[]{:S(2)}, u32[]{:S(2)}) collective-permute-start(f32[16,256]{1,0:T(8,128)S(1)} %get-tuple-element.32), channel_id=1, source_target_pairs={{4,0},{5,1},{6,2},{7,3},{12,8},{13,9},{14,10},{15,11},{20,16},{21,... | collective-permute-start | bytes 49160 | tf_op jit(solution)/shard_map/ppermute | solution.py:19
  99.1 14.0 %collective-permute-start.1 = (f32[16,256]{1,0:T(8,128)S(1)}, f32[16,256]{1,0:T(8,128)S(1)}, u32[]{:S(2)}, u32[]{:S(2)}) collective-permute-start(f32[16,256]{1,0:T(8,128)S(1)} %get-tuple-element.33), channel_id=1, source_target_pairs={{0,4},{1,5},{2,6},{3,7},{8,12},{9,13},{10,14},{11,15},{16,20},{17,... | collective-permute-start | bytes 49160 | tf_op jit(solution)/shard_map/ppermute | solution.py:19
  103.9 7.0 %copy-start.5 = (s32[1,1,256,256]{3,2,1,0:T(8,128)S(1)}, s32[1,1,256,256]{3,2,1,0:T(8,128)}, u32[]{:S(2)}) copy-start(s32[1,1,256,256]{3,2,1,0:T(8,128)} %param.16) | copy-start | bytes 786436
  120.7 3.7 %copy-start.3 = (f32[1,16,1,256,256]{3,4,1,2,0:T(8,128)S(1)}, f32[1,16,1,256,256]{3,4,1,2,0:T(8,128)}, u32[]{:S(2)}) copy-start(f32[1,16,1,256,256]{3,4,1,2,0:T(8,128)} %copy.121) | copy-start | bytes 12582916
  133.7 2.0 copy-start.1
  136.6 100.5 %reduce-scatter.5.cloned.1.call-start = ((), (), s32[]{:S(2)}) async-start(), calls=%async_computation.3 | async-start | bytes 2359296 | tf_op jit(solution)/shard_map/reduce_scatter | solution.py:64
  146.9 48.9 %collective-permute-start.10 = (f32[8,256,256]{1,2,0:T(8,128)}, f32[8,256,256]{1,2,0:T(8,128)}, u32[]{:S(2)}, u32[]{:S(2)}) collective-permute-start(f32[8,256,256]{1,2,0:T(8,128)} %copy.144), channel_id=1, source_target_pairs={{8,0},{16,8},{24,16},{9,1},{17,9},{25,17},{10,2},{18,10},{26,18},{... | collective-permute-start | bytes 6291464 | tf_op jit(solution)/shard_map/ppermute | solution.py:19
  195.8 45.6 %collective-permute-start.11 = (f32[8,256,256]{2,1,0:T(8,128)}, f32[8,256,256]{2,1,0:T(8,128)}, u32[]{:S(2)}, u32[]{:S(2)}) collective-permute-start(f32[8,256,256]{2,1,0:T(8,128)} %all-gather.4.cloned.1.call-done), channel_id=1, source_target_pairs={{0,8},{8,16},{16,24},{1,9},{9,17},{17,25},{2,10},{10,18},{18,26},{... | collective-permute-start | bytes 6291464 | tf_op jit(solution)/shard_map/ppermute | solution.py:19
  201.4 12.9 %collective-permute-start.9 = (f32[16,256]{1,0:T(8,128)S(1)}, f32[16,256]{1,0:T(8,128)S(1)}, u32[]{:S(2)}, u32[]{:S(2)}) collective-permute-start(f32[16,256]{1,0:T(8,128)S(1)} %bitcast.94), channel_id=1, source_target_pairs={{0,1},{1,2},{2,3},{3,4},{4,5},{5,6},{6,7},{8,9},{9,10},{10,11},{11... | collective-permute-start | bytes 49160 | tf_op jit(solution)/shard_map/ppermute | solution.py:19
  207.1 7.2 %collective-permute-start.6 = (f32[16,256]{1,0:T(8,128)S(1)}, f32[16,256]{1,0:T(8,128)S(1)}, u32[]{:S(2)}, u32[]{:S(2)}) collective-permute-start(f32[16,256]{1,0:T(8,128)S(1)} %get-tuple-element.30), channel_id=1, source_target_pairs={{4,0},{5,1},{6,2},{7,3},{12,8},{13,9},{14,10},{15,11},{20,16},{21,... | collective-permute-start | bytes 49160 | tf_op jit(solution)/shard_map/ppermute | solution.py:19
  208.4 7.9 %collective-permute-start.7 = (f32[16,256]{1,0:T(8,128)S(1)}, f32[16,256]{1,0:T(8,128)S(1)}, u32[]{:S(2)}, u32[]{:S(2)}) collective-permute-start(f32[16,256]{1,0:T(8,128)S(1)} %get-tuple-element.31), channel_id=1, source_target_pairs={{0,4},{1,5},{2,6},{3,7},{8,12},{9,13},{10,14},{11,15},{16,20},{17,... | collective-permute-start | bytes 49160 | tf_op jit(solution)/shard_map/ppermute | solution.py:19
  213.0 5.4 %collective-permute-start.8 = (f32[16,256]{1,0:T(8,128)S(1)}, f32[16,256]{1,0:T(8,128)S(1)}, u32[]{:S(2)}, u32[]{:S(2)}) collective-permute-start(f32[16,256]{1,0:T(8,128)S(1)} %bitcast.93), channel_id=1, source_target_pairs={{1,0},{2,1},{3,2},{4,3},{5,4},{6,5},{7,6},{9,8},{10,9},{11,10},{12... | collective-permute-start | bytes 49160 | tf_op jit(solution)/shard_map/ppermute | solution.py:19
  244.6 3.7 %copy-start.2 = (f32[16,256,256]{1,2,0:T(8,128)S(1)}, f32[16,256,256]{1,2,0:T(8,128)}, u32[]{:S(2)}) copy-start(f32[16,256,256]{1,2,0:T(8,128)} %copy-done.1) | copy-start | bytes 12582916
Sparse Core Ops, SparseCore 0:
  9.3 30.5 all-gather.5
  69.6 41.9 reduce-scatter.2
  136.8 29.0 all-gather.3
  195.9 41.2 reduce-scatter.4
where the time goes:
time: 271 us; the launch traced here: 270 us
  waiting for transfers between devices  121 us (45%)
  local copies, waits for them, and re-layouts  61 us (23%)
  starting transfers between devices  31.2 us (12%)
  matrix products  21.7 us (8%)
  other arithmetic  21.5 us (8%)
  between operations  14.3 us (5%)
    ppermute x12, waiting for transfers between devices, shifted(): lax.ppermute(value, axis, [(source, source + steps) for source in range(i...  102 us
    ppermute x12, starting transfers between devices, shifted(): lax.ppermute(value, axis, [(source, source + steps) for source in range(i...  31.1 us
    reduce_scatter x2, waiting for transfers between devices, on_device(): lax.psum_scatter(terms_above, 'tile', scatter_dimension=0, tiled=True)[0]  18.7 us
    unnamed x22, local copies, waits for them, and re-layouts  18.3 us
    sub x2, other arithmetic, on_device(): change = lapl + over + under - 2.0 * field - speed * (field - under)  15.3 us
    slice x2, local copies, waits for them, and re-layouts, on_device(): field[:, 0, :]  8.12 us
    dot_general x4, matrix products, on_device(): jnp.einsum('kba,bc,kcd->kad', blocks_x, bottom_plane, blocks_y, precision...  7.82 us
    dot_general x4, matrix products, on_device(): jnp.einsum('kab,kbc,kdc->ad', blocks_x, picked, blocks_y, precision=HIGHEST)  7.41 us
  transfers between devices with their start and end apart: 16, of which 5 were waited for; matrix products, arithmetic and copies ran while one was open for 22% of the time, Pallas kernels for 0%

commit v1 on v0

v1 whole, which is shorter than its diff:
```python
import functools

import jax
import jax.numpy as jnp
from jax import lax
from jax.experimental import pallas as pl
from jax.experimental.pallas import tpu as pltpu
from jax.sharding import PartitionSpec as P

TCOL = 4
STEPS = 2
TIME_STEP = 0.1
INJECT_RATE = 2.0
AMBIENT = 1.0
MESH = pl.DeviceIdType.MESH
CHUNKS = 4
STRIP = 32
LANES = 128
ALL, INNER, TOP, BOTTOM = 0, 1, 2, 3
F32 = jnp.float32
BF16 = jnp.bfloat16


def split(value):
    high = value.astype(BF16)
    return high, (value - high.astype(F32)).astype(BF16)


def left_cat(value):
    high, low = split(value)
    return jnp.concatenate([high, low, high], axis=1)


def right_cat(value):
    high, low = split(value)
    return jnp.concatenate([high, high, low], axis=0)


def dot(left, right):
    return jnp.dot(left, right, preferred_element_type=F32)


def kernel(
    tiles, lifts, nb,
    sources_ref, spacing_ref, oxygen, velocity, inlets, proj_x, proj_y, out,
    f0, f1, f2, vel, inl, xw, yw,
    x_cat, xt_cat, y_cat, yt_cat, halves, pieces,
    tops_0, tops_1, acc, core_in, above_in, send_down, gbelow,
    hs, hr, hcol,
    load_sems, out_sems, halo_ss, halo_rs,
    ag_ss, ag_rs, rs_ss, rs_rs, z_ss, z_rs, hcol_in, *stage_in
):
    depth, cx, cy = f0.shape
    kk = xw.shape[0]
    rows = cx // CHUNKS
    tops = (tops_0, tops_1)
    tile = lax.axis_index("tile")
    lift = lax.axis_index("lift")
    column = tile % TCOL
    base = tile - column
    row_down = (tile + TCOL) % tiles
    row_up = (tile + tiles - TCOL) % tiles
    col_right = base + (column + 1) % TCOL
    col_left = base + (column + TCOL - 1) % TCOL
    has_above = lift < lifts - 1
    has_below = lift > 0

    def flipped(bit):
        size = 1 << bit
        return tile + size * (1 - 2 * ((tile // size) % 2))

    partner_core = flipped(0)
    partner = [flipped(nb - axis) for axis in range(nb)]

    bottom_load = pltpu.make_async_copy(oxygen.at[0], f0.at[0], load_sems.at[0])
    x_load = pltpu.make_async_copy(proj_x, xw, load_sems.at[1])
    y_load = pltpu.make_async_copy(proj_y, yw, load_sems.at[2])
    f_load = pltpu.make_async_copy(oxygen.at[pl.ds(1, depth - 1)], f0.at[pl.ds(1, depth - 1)], load_sems.at[3])
    v_load = pltpu.make_async_copy(velocity, vel, load_sems.at[4])
    i_load = pltpu.make_async_copy(inlets, inl, load_sems.at[5])
    for load in (bottom_load, x_load, y_load, f_load, v_load, i_load):
        load.start()

    barrier = pltpu.get_barrier_semaphore()
    peers = [partner_core] + partner + [row_down, row_up, col_right, col_left]
    for peer in peers:
        pl.semaphore_signal(barrier, inc=1, device_id={"tile": peer}, device_id_type=MESH)

    @pl.when(has_above)
    def _():
        pl.semaphore_signal(barrier, inc=1, device_id={"lift": lift + 1}, device_id_type=MESH)

    @pl.when(has_below)
    def _():
        pl.semaphore_signal(barrier, inc=1, device_id={"lift": lift - 1}, device_id_type=MESH)

    pl.semaphore_wait(barrier, len(peers) + has_above.astype(jnp.int32) + has_below.astype(jnp.int32))

    def cut(c):
        return pl.ds(c * rows, rows)

    def order(c):
        axes = list(range(nb))
        return axes if c % 2 == 0 else axes[::-1]

    def remote(src, dst, ss, rs, **where):
        return pltpu.make_async_remote_copy(
            src_ref=src, dst_ref=dst, send_sem=ss, recv_sem=rs, device_id=where, device_id_type=MESH
        )

    def top_up(s, c):
        field = oxygen if s == 0 else f1
        return remote(
            field.at[depth - 1, cut(c)],
            tops[s].at[(0,) + (0,) * nb + (cut(c),)],
            z_ss.at[s, 0, c], z_rs.at[s, 0, c], lift=lift + 1,
        )

    def spread(s, c, stage):
        if stage == nb:
            every = (slice(None),) * nb
            return remote(
                tops[s].at[(0,) + every + (cut(c),)], tops[s].at[(1,) + every + (cut(c),)],
                ag_ss.at[s, stage, c], ag_rs.at[s, stage, c], tile=partner_core,
            )
        axes = order(c)
        index = [0] * nb
        for axis in axes[:stage]:
            index[axis] = slice(None)
        there = list(index)
        there[axes[stage]] = 1
        return remote(
            tops[s].at[(0,) + tuple(index) + (cut(c),)], tops[s].at[(0,) + tuple(there) + (cut(c),)],
            ag_ss.at[s, stage, c], ag_rs.at[s, stage, c], tile=partner[axes[stage]],
        )

    def top_arrived(s, c):
        @pl.when(has_below)
        def _():
            top_up(s, c).wait_recv()

        @pl.when(lift == 0)
        def _():
            tops[s][(0,) + (0,) * nb + (cut(c),)] = jnp.zeros((rows, cy), F32)

    def reduce_core(s, c):
        every = (slice(None),) * nb
        return remote(
            acc.at[(s, 1) + every + (cut(c),)], core_in.at[(s,) + every + (cut(c),)],
            rs_ss.at[s, nb, c], rs_rs.at[s, nb, c], tile=partner_core,
        )

    def left_index(c, stage):
        axes = order(c)
        index = [slice(None)] * nb
        for axis in axes[:stage]:
            index[axis] = 0
        return index

    def reduce_stage(s, c, stage):
        axis = order(c)[stage]
        index = left_index(c, stage)
        index[axis] = 1
        every = (slice(None),) * (nb - 1 - stage)
        return remote(
            acc.at[(s, 0) + tuple(index) + (cut(c),)], stage_in[stage].at[(s,) + every + (cut(c),)],
            rs_ss.at[s, stage, c], rs_rs.at[s, stage, c], tile=partner[axis],
        )

    def add_core(s, c):
        reduce_core(s, c).wait_recv()
        every = (slice(None),) * nb
        at = (s, 0) + every + (cut(c),)
        acc[at] = acc[at] + core_in[(s,) + every + (cut(c),)]

    def add_stage(s, c, stage):
        reduce_stage(s, c, stage).wait_recv()
        index = tuple(left_index(c, stage + 1))
        at = (s, 0) + index + (cut(c),)
        every = (slice(None),) * (nb - 1 - stage)
        total = acc[at] + stage_in[stage][(s,) + every + (cut(c),)]
        if stage == nb - 1:
            send_down[s, cut(c)] = total
        else:
            acc[at] = total

    def sum_down(s, c):
        return remote(
            send_down.at[s, cut(c)], above_in.at[s, cut(c)],
            z_ss.at[s, 1, c], z_rs.at[s, 1, c], lift=lift - 1,
        )

    def ghost_above(s, c):
        @pl.when(has_above)
        def _():
            sum_down(s, c).wait_recv()

        @pl.when(lift == lifts - 1)
        def _():
            above_in[s, cut(c)] = jnp.full((rows, cy), AMBIENT, F32)

        return above_in[s, cut(c)]

    def if_below(copy_of, s, c, action):
        @pl.when(has_below)
        def _():
            getattr(copy_of(s, c), action)()

    def if_above(copy_of, s, c, action):
        @pl.when(has_above)
        def _():
            getattr(copy_of(s, c), action)()

    for c in range(CHUNKS):
        if_above(top_up, 0, c, "start")

    lane = lax.broadcasted_iota(jnp.int32, (STRIP, LANES), 1)
    halo_to = [row_down, row_up, col_right, col_left]

    def halo_copy(g, d):
        return remote(hs.at[g, d], hr.at[g, d], halo_ss.at[g, d], halo_rs.at[g, d], tile=halo_to[d])

    def halo_send(src, g, first, end):
        for z in range(first, end):
            hs[g, 0, z:z + 1, :] = src[z, cx - 1:cx, :]
            hs[g, 1, z:z + 1, :] = src[z, 0:1, :]

        def one(i, carry):
            at = pl.ds(pl.multiple_of(i * STRIP, STRIP), STRIP)
            right = jnp.zeros((STRIP, LANES), F32)
            left = jnp.zeros((STRIP, LANES), F32)
            for z in range(first, end):
                right = jnp.where(lane == z, pltpu.roll(src[z, at, cy - LANES:], (z + 1) % LANES, 1), right)
                rim = src[z, at, :LANES]
                left = jnp.where(lane == z, pltpu.roll(rim, z, 1) if z else rim, left)
            hcol[0, at] = right
            hcol[1, at] = left
            return carry

        lax.fori_loop(0, cx // STRIP, one, 0)
        hs[g, 2] = hcol[0].T[:depth]
        hs[g, 3] = hcol[1].T[:depth]
        for d in range(4):
            halo_copy(g, d).start()

    at_edge = [base == 0, base == tiles - TCOL, column == 0, column == TCOL - 1]

    def halo_receive(g):
        for d in range(4):
            halo_copy(g, d).wait_recv()
        for d in range(2):
            hr[g, d] = jnp.where(at_edge[d], 0.0, hr[g, d])
        for d in (2, 3):
            value = jnp.where(at_edge[d], 0.0, hr[g, d])
            padded = jnp.concatenate([value, jnp.zeros((LANES - depth, cx), F32)], axis=0)
            hcol_in[g, d - 2] = padded.T


    inverse = 1.0 / (spacing_ref[0] * spacing_ref[0])
    row_at = lax.broadcasted_iota(jnp.int32, (STRIP, cy), 0)
    strips = range(0, cx, STRIP)

    def stencil(src, z, g, r, under, over):
        at = pl.ds(r, STRIP)
        here = src[z, at]
        before = hr[g, 0, pl.ds(z, 1), :] if r == 0 else src[z, pl.ds(r - 1, 1), :]
        after = hr[g, 1, pl.ds(z, 1), :] if r == cx - STRIP else src[z, pl.ds(r + STRIP, 1), :]
        north = jnp.where(row_at == 0, before, pltpu.roll(here, 1, 0))
        south = jnp.where(row_at == STRIP - 1, after, pltpu.roll(here, STRIP - 1, 0))
        west = pltpu.roll(here, 1, 1)
        east = pltpu.roll(here, cy - 1, 1)
        west_rim = pltpu.roll(hcol_in[g, 0, at], (LANES - z) % LANES, 1)
        east_rim = pltpu.roll(hcol_in[g, 1, at], LANES - 1 - z, 1)
        west = jnp.concatenate([jnp.where(lane == 0, west_rim, west[:, :LANES]), west[:, LANES:]], axis=1)
        east = jnp.concatenate(
            [east[:, : cy - LANES], jnp.where(lane == LANES - 1, east_rim, east[:, cy - LANES:])], axis=1
        )
        change = (north + south + west + east - 4.0 * here) * inverse - 2.0 * here
        speed = vel[z, at]
        if under is None:
            change = change - speed * here
        else:
            below = src[under, at]
            change = change + below - speed * (here - below)
        if over is not None:
            change = change + src[over, at]
        return here, change

    def inner(src, dst, g, first, end):
        def one(z, carry):
            for r in strips:
                here, change = stencil(src, z, g, r, z - 1, z + 1)
                dst[z, pl.ds(r, STRIP)] = here + TIME_STEP * change
            return carry

        lax.fori_loop(first, end, one, 0)

    def top_part(src, dst, g):
        for r in strips:
            here, change = stencil(src, depth - 1, g, r, depth - 2, None)
            dst[depth - 1, pl.ds(r, STRIP)] = here + TIME_STEP * change

    def bottom_part(src, dst, g):
        for r in strips:
            at = pl.ds(r, STRIP)
            here, change = stencil(src, 0, g, r, None, 1)
            change = change + INJECT_RATE * inl[at].astype(F32) * (1.0 - here)
            dst[0, at] = here + TIME_STEP * change

    def top_add(s, dst, c):
        dst[depth - 1, cut(c)] = dst[depth - 1, cut(c)] + TIME_STEP * ghost_above(s, c)

    def bottom_add(s, dst):
        for r in strips:
            at = pl.ds(r, STRIP)
            ghost = jnp.where(has_below, gbelow[at], 0.0)
            dst[0, at] = dst[0, at] + TIME_STEP * ((1.0 + vel[0, at]) * ghost)

    def prepare_down():
        x_load.wait()
        y_load.wait()
        for k in range(kk):
            xt_cat[pl.ds(k * cx, cx)] = left_cat(xw[k].T)
            y_cat[k] = right_cat(yw[k])

    def prepare_up():
        for k in range(kk):
            x_cat[k] = left_cat(xw[k])
            yt_cat[pl.ds(3 * k * cy, 3 * cy)] = right_cat(yw[k].T)

    def project_down(plane):
        field = right_cat(plane)
        for k in range(kk):
            half = left_cat(dot(xt_cat[pl.ds(k * cx, cx)], field))
            pieces[k] = dot(half, y_cat[k])

    size_of = [1] + [1 << (nb - axis) for axis in range(nb)]

    def slot_tile(bits):
        there = tile
        for bit, size in zip(bits, size_of):
            if bit:
                there = there + size * (1 - 2 * ((tile // size) % 2))
        return there

    all_slots = [[slot % 2] + [(slot >> (nb - axis)) % 2 for axis in range(nb)] for slot in range(tiles)]
    listed = [sources_ref[0, 0, k] for k in range(kk)]
    wanted = [[listed[k] == slot_tile(bits) for k in range(kk)] for bits in all_slots]

    def fill(s, c):
        for r in range(0, rows, STRIP):
            at = pl.ds(c * rows + r, STRIP)
            values = [pieces[k, at] for k in range(kk)]
            for slot, bits in enumerate(all_slots):
                total = values[0] if slot == tiles // 2 else None
                for k in range(1, kk):
                    term = jnp.where(wanted[slot][k], values[k], 0.0)
                    total = term if total is None else total + term
                acc[(s,) + tuple(bits) + (at,)] = total

    def project_up(s):
        for k in range(kk):
            at = tuple((listed[k] // size + tile // size) % 2 for size in size_of)
            half = dot(x_cat[k], right_cat(tops[s][at]))
            halves[:, pl.ds(3 * k * cy, 3 * cy)] = left_cat(half)
        gbelow[...] = dot(halves[...], yt_cat[...])

    def put(z0, n, i):
        return pltpu.make_async_copy(f2.at[pl.ds(z0, n)], out.at[pl.ds(z0, n)], out_sems.at[i])

    def reduce_pipeline(s, between):
        for turn in range(CHUNKS + nb + 1):
            if turn < CHUNKS:
                fill(s, turn)
                reduce_core(s, turn).start()
            c = turn - 1
            if 0 <= c < CHUNKS:
                add_core(s, c)
                reduce_stage(s, c, 0).start()
            for stage in range(nb):
                c = turn - 2 - stage
                if 0 <= c < CHUNKS:
                    add_stage(s, c, stage)
                    if stage == nb - 1:
                        if_below(sum_down, s, c, "start")
                    else:
                        reduce_stage(s, c, stage + 1).start()
            between(turn)

    def spread_turn(s, turn):
        c = turn
        if 0 <= c < CHUNKS:
            top_arrived(s, c)
            spread(s, c, 0).start()
        for stage in range(nb + 1):
            c = turn - 1 - stage
            if 0 <= c < CHUNKS:
                spread(s, c, stage).wait_recv()
                if stage < nb:
                    spread(s, c, stage + 1).start()

    spread_turns = CHUNKS + nb + 1

    prepare_down()
    bottom_load.wait()
    project_down(f0[0])

    hs[...] = jnp.zeros_like(hs)

    def between_first(turn):
        if turn >= CHUNKS:
            spread_turn(0, turn - CHUNKS)
        if turn == 0:
            f_load.wait()
            halo_send(f0, ALL, 0, depth)
        if turn == 1:
            prepare_up()
        if turn == 3:
            v_load.wait()
            i_load.wait()
            halo_receive(ALL)
            top_part(f0, f1, ALL)
        if turn == 4:
            bottom_part(f0, f1, ALL)
        if turn == 5:
            inner(f0, f1, ALL, 1, 3)

    reduce_pipeline(0, between_first)

    for turn in range(CHUNKS):
        spread_turn(0, turn + nb + 1)
        top_add(0, f1, turn)
        if_above(top_up, 1, turn, "start")
        inner(f0, f1, ALL, 3 + 3 * turn, 6 + 3 * turn)

    spread_turn(1, 0)
    spread_turn(1, 1)
    project_up(0)
    bottom_add(0, f1)
    spread_turn(1, 2)
    project_down(f1[0])
    spread_turn(1, 3)
    halo_send(f1, INNER, 1, depth - 1)
    halo_send(f1, TOP, depth - 1, depth)
    halo_send(f1, BOTTOM, 0, 1)
    spread_turn(1, 4)

    def between_second(turn):
        if 5 + turn < spread_turns:
            spread_turn(1, 5 + turn)
        if turn == 2:
            halo_receive(INNER)
            inner(f1, f2, INNER, 1, 5)
        if turn == 3:
            project_up(1)
            halo_receive(BOTTOM)
            bottom_part(f1, f2, BOTTOM)
            bottom_add(1, f2)
        if turn == 4:
            halo_receive(TOP)
            top_part(f1, f2, TOP)
            inner(f1, f2, INNER, 5, 8)
            put(0, 8, 0).start()
        if turn == 5:
            inner(f1, f2, INNER, 8, 12)
        if turn == 6:
            inner(f1, f2, INNER, 12, depth - 1)
            put(8, depth - 9, 1).start()

    reduce_pipeline(1, between_second)
    for c in range(CHUNKS):
        top_add(1, f2, c)
    put(depth - 1, 1, 2).start()

    for s in range(STEPS):
        for c in range(CHUNKS):
            if_above(top_up, s, c, "wait_send")
            if_below(sum_down, s, c, "wait_send")
            reduce_core(s, c).wait_send()
            for stage in range(nb):
                reduce_stage(s, c, stage).wait_send()
            for stage in range(nb + 1):
                spread(s, c, stage).wait_send()
    for g in range(4):
        for d in range(4):
            halo_copy(g, d).wait_send()
    put(0, 8, 0).wait()
    put(8, depth - 9, 1).wait()
    put(depth - 1, 1, 2).wait()


def on_device(tiles, lifts, oxygen, velocity, spacing, inlets, proj_x, proj_y, sources):
    nb = tiles.bit_length() - 2
    field = oxygen[0, :, 0]
    speed = velocity[0, :, 0]
    depth, cx, cy = field.shape
    kk = proj_x.shape[2]
    two = (2,) * nb
    any_spec = pl.BlockSpec(memory_space=pl.ANY)
    smem = pl.BlockSpec(memory_space=pltpu.SMEM)
    plane = (cx, cy)
    dma = pltpu.SemaphoreType.DMA
    result = pl.pallas_call(
        functools.partial(kernel, tiles, lifts, nb),
        out_shape=jax.ShapeDtypeStruct(field.shape, F32),
        in_specs=[smem, smem] + [any_spec] * 5,
        out_specs=any_spec,
        scratch_shapes=[
            pltpu.VMEM(field.shape, F32),
            pltpu.VMEM(field.shape, F32),
            pltpu.VMEM(field.shape, F32),
            pltpu.VMEM(field.shape, F32),
            pltpu.VMEM(plane, jnp.int32),
            pltpu.VMEM((kk,) + plane, F32),
            pltpu.VMEM((kk,) + plane, F32),
        ]
        + [
            pltpu.VMEM((kk, cx, 3 * cx), BF16),
            pltpu.VMEM((kk * cx, 3 * cx), BF16),
            pltpu.VMEM((kk, 3 * cy, cy), BF16),
            pltpu.VMEM((3 * kk * cy, cy), BF16),
            pltpu.VMEM((cx, 3 * kk * cy), BF16),
            pltpu.VMEM((kk,) + plane, F32),
            pltpu.VMEM((2,) + two + plane, F32),
            pltpu.VMEM((2,) + two + plane, F32),
            pltpu.VMEM((STEPS, 2) + two + plane, F32),
            pltpu.VMEM((STEPS,) + two + plane, F32),
            pltpu.VMEM((STEPS,) + plane, F32),
            pltpu.VMEM((STEPS,) + plane, F32),
            pltpu.VMEM(plane, F32),
            pltpu.VMEM((4, 4, depth, cx), F32),
            pltpu.VMEM((4, 4, depth, cx), F32),
            pltpu.VMEM((2, cx, LANES), F32),
            dma((6,)),
            dma((3,)),
            dma((4, 4)),
            dma((4, 4)),
            dma((STEPS, nb + 1, CHUNKS)),
            dma((STEPS, nb + 1, CHUNKS)),
            dma((STEPS, nb + 1, CHUNKS)),
            dma((STEPS, nb + 1, CHUNKS)),
            dma((STEPS, 2, CHUNKS)),
            dma((STEPS, 2, CHUNKS)),
            pltpu.VMEM((4, 2, cx, LANES), F32),
        ]
        + [pltpu.VMEM((STEPS,) + (2,) * (nb - 1 - stage) + plane, F32) for stage in range(nb)],
        compiler_params=pltpu.CompilerParams(
            collective_id=0, has_side_effects=True, vmem_limit_bytes=60 * 1024 * 1024
        ),
        cost_estimate=pl.CostEstimate(flops=10**9, bytes_accessed=16 * 1024 * 1024, transcendentals=0),
    )(sources, spacing, field, speed, inlets[0, 0], proj_x[0, 0], proj_y[0, 0])
    return result[None, :, None]


def solution(mesh):
    return jax.shard_map(
        functools.partial(on_device, mesh.shape["tile"], mesh.shape["lift"]),
        mesh=mesh,
        in_specs=(
            P("lift", None, "tile", None, None),
            P("lift", None, "tile", None, None),
            P("lift"),
            P("lift", "tile", None, None),
            P("lift", "tile", None, None, None),
            P("lift", "tile", None, None, None),
            P("lift", "tile", None),
        ),
        out_specs=P("lift", None, "tile", None, None),
        check_vma=False,
    )
```

time: 271 us -> 85 us (0.31)
  waiting for transfers between devices: 121 us -> 0 us
  Pallas kernels: 0 us -> 79.6 us
  local copies, waits for them, and re-layouts: 61 us -> 4.6 us
  starting transfers between devices: 31.2 us -> 0 us
  matrix products: 21.7 us -> 0 us
  other arithmetic: 21.5 us -> 0 us
  between operations: 14.3 us -> 0.66 us
    ppermute x12 -> x0, waiting for transfers between devices: 102 us -> none  [shifted(): lax.ppermute(value, axis, [(source, source + steps) for source in range(i...]
    pallas_call x0 -> x1, Pallas kernels: none -> 79.6 us  [on_device(): pl.pallas_call(functools.partial(kernel, tiles, lifts, nb), out_shape=jax...]
    ppermute x12 -> x0, starting transfers between devices: 31.1 us -> none  [shifted(): lax.ppermute(value, axis, [(source, source + steps) for source in range(i...]
    dot_general x10 -> x0, matrix products: 21.7 us -> none  [the longest x4 7.82 us: on_device(): jnp.einsum('kba,bc,kcd->kad', blocks_x, bottom_plane, blocks_y, precision...]
    reduce_scatter x2 -> x0, waiting for transfers between devices: 18.7 us -> none  [on_device(): lax.psum_scatter(terms_above, 'tile', scatter_dimension=0, tiled=True)[0]]
    slice x7 -> x0, local copies, waits for them, and re-layouts: 17 us -> none  [the longest x2 8.12 us: on_device(): field[:, 0, :]]
    sub x2 -> x0, other arithmetic: 15.3 us -> none  [on_device(): change = lapl + over + under - 2.0 * field - speed * (field - under)]
    unnamed x22 -> x1, local copies, waits for them, and re-layouts: 18.3 us -> 4.6 us
  transfers between devices with their start and end apart: 16 -> 0, of which waited for: 5 -> 0; matrix products, arithmetic and copies ran while one was open for 22% -> 0% of each run, Pallas kernels for 0% -> 0%
where the time goes in v1:
time: 85 us; the launch traced here: 84.9 us
  Pallas kernels  79.6 us (94%)
  local copies, waits for them, and re-layouts  4.6 us (5%)
    pallas_call x1, Pallas kernels, on_device(): pl.pallas_call(functools.partial(kernel, tiles, lifts, nb), out_shape=jax...  79.6 us
    unnamed x1, local copies, waits for them, and re-layouts  4.6 us

profile of v1, /device:TPU:0, one launch (start us, length us, event | category | flops | bytes accessed | tf_op | source)
XLA Modules:
  0.0 84.9 jit_solution(9103119249528974133)
XLA Ops:
  0.7 79.6 %shard_map.73 = f32[16,256,256]{2,1,0:T(8,128)} custom-call(s32[1,1,4]{2,1,0:T(1,128)} %sources_ref.1, f32[1]{0:T(128)S(6)} %copy.10.spacing_ref, f32[16,256,256]{2,1,0:T(8,128)} %bitcast.9, f32[16,256,256]{2,1,0:T(8,128)} %bitcast.10, s32[256,256]{1,0:T(8,128)} %bitcast.13, f32[4,256,256]{2,1,0:T(8,128)} %bitcast.11, f32[4,256,256]{2,1,0:T(8,128)} %bitcast.12), custom_call_target="tpu_custom_call" | custom-call | flops 1000000000 | bytes 16777216 | tf_op jit(solution)/shard_map/pallas_call | solution.py:503
  80.3 4.6 %copy.11 = f32[1,16,1,256,256]{4,3,2,1,0:T(8,128)} copy(f32[1,16,1,256,256]{4,3,2,1,0:T(8,128)} %bitcast.8) | data formatting | bytes 8388608

commit v2 on v1

--- a/solution.py
+++ b/solution.py
@@ -368,107 +368,92 @@
     def put(z0, n, i):
         return pltpu.make_async_copy(f2.at[pl.ds(z0, n)], out.at[pl.ds(z0, n)], out_sems.at[i])
 
-    def reduce_pipeline(s, between):
-        for turn in range(CHUNKS + nb + 1):
-            if turn < CHUNKS:
-                fill(s, turn)
-                reduce_core(s, turn).start()
-            c = turn - 1
-            if 0 <= c < CHUNKS:
-                add_core(s, c)
-                reduce_stage(s, c, 0).start()
-            for stage in range(nb):
-                c = turn - 2 - stage
-                if 0 <= c < CHUNKS:
-                    add_stage(s, c, stage)
-                    if stage == nb - 1:
-                        if_below(sum_down, s, c, "start")
-                    else:
-                        reduce_stage(s, c, stage + 1).start()
-            between(turn)
-
-    def spread_turn(s, turn):
-        c = turn
-        if 0 <= c < CHUNKS:
+    chunks = range(CHUNKS)
+
+    def reduce_enter(s):
+        for c in chunks:
+            fill(s, c)
+            reduce_core(s, c).start()
+
+    def reduce_cores(s):
+        for c in chunks:
+            add_core(s, c)
+            reduce_stage(s, c, 0).start()
+
+    def reduce_next(s, stage):
+        for c in chunks:
+            add_stage(s, c, stage)
+            if stage == nb - 1:
+                if_below(sum_down, s, c, "start")
+            else:
+                reduce_stage(s, c, stage + 1).start()
+
+    def spread_enter(s):
+        for c in chunks:
             top_arrived(s, c)
             spread(s, c, 0).start()
-        for stage in range(nb + 1):
-            c = turn - 1 - stage
-            if 0 <= c < CHUNKS:
-                spread(s, c, stage).wait_recv()
-                if stage < nb:
-                    spread(s, c, stage + 1).start()
-
-    spread_turns = CHUNKS + nb + 1
+
+    def spread_next(s, stage):
+        for c in chunks:
+            spread(s, c, stage).wait_recv()
+            if stage < nb:
+                spread(s, c, stage + 1).start()
 
     prepare_down()
     bottom_load.wait()
     project_down(f0[0])
-
+    reduce_enter(0)
     hs[...] = jnp.zeros_like(hs)
-
-    def between_first(turn):
-        if turn >= CHUNKS:
-            spread_turn(0, turn - CHUNKS)
-        if turn == 0:
-            f_load.wait()
-            halo_send(f0, ALL, 0, depth)
-        if turn == 1:
-            prepare_up()
-        if turn == 3:
-            v_load.wait()
-            i_load.wait()
-            halo_receive(ALL)
-            top_part(f0, f1, ALL)
-        if turn == 4:
+    f_load.wait()
+    halo_send(f0, ALL, 0, depth)
+    reduce_cores(0)
+    spread_enter(0)
+    prepare_up()
+    v_load.wait()
+    i_load.wait()
+    halo_receive(ALL)
+    top_part(f0, f1, ALL)
+    for stage in range(nb):
+        reduce_next(0, stage)
+        spread_next(0, stage)
+        if stage == 0:
             bottom_part(f0, f1, ALL)
-        if turn == 5:
             inner(f0, f1, ALL, 1, 3)
-
-    reduce_pipeline(0, between_first)
-
-    for turn in range(CHUNKS):
-        spread_turn(0, turn + nb + 1)
-        top_add(0, f1, turn)
-        if_above(top_up, 1, turn, "start")
-        inner(f0, f1, ALL, 3 + 3 * turn, 6 + 3 * turn)
-
-    spread_turn(1, 0)
-    spread_turn(1, 1)
+    inner(f0, f1, ALL, 3, 7)
+
+    for c in chunks:
+        top_add(0, f1, c)
+        if_above(top_up, 1, c, "start")
+        inner(f0, f1, ALL, 7 + 2 * c, 9 + 2 * c)
+    spread_next(0, nb)
     project_up(0)
     bottom_add(0, f1)
-    spread_turn(1, 2)
+    spread_enter(1)
     project_down(f1[0])
-    spread_turn(1, 3)
+    reduce_enter(1)
     halo_send(f1, INNER, 1, depth - 1)
     halo_send(f1, TOP, depth - 1, depth)
     halo_send(f1, BOTTOM, 0, 1)
-    spread_turn(1, 4)
-
-    def between_second(turn):
-        if 5 + turn < spread_turns:
-            spread_turn(1, 5 + turn)
-        if turn == 2:
-            halo_receive(INNER)
-            inner(f1, f2, INNER, 1, 5)
-        if turn == 3:
-            project_up(1)
+    reduce_cores(1)
+    spread_next(1, 0)
+    halo_receive(INNER)
+    inner(f1, f2, INNER, 1, 3)
+    for stage in range(nb):
+        reduce_next(1, stage)
+        spread_next(1, stage + 1)
+        if stage == 0:
             halo_receive(BOTTOM)
             bottom_part(f1, f2, BOTTOM)
-            bottom_add(1, f2)
-        if turn == 4:
             halo_receive(TOP)
             top_part(f1, f2, TOP)
-            inner(f1, f2, INNER, 5, 8)
-            put(0, 8, 0).start()
-        if turn == 5:
-            inner(f1, f2, INNER, 8, 12)
-        if turn == 6:
-            inner(f1, f2, INNER, 12, depth - 1)
-            put(8, depth - 9, 1).start()
-
-    reduce_pipeline(1, between_second)
-    for c in range(CHUNKS):
+            inner(f1, f2, INNER, 3, 6)
+    project_up(1)
+    bottom_add(1, f2)
+    inner(f1, f2, INNER, 6, 8)
+    put(0, 8, 0).start()
+    inner(f1, f2, INNER, 8, depth - 1)
+    put(8, depth - 9, 1).start()
+    for c in chunks:
         top_add(1, f2, c)
     put(depth - 1, 1, 2).start()
 

time: 85 us -> 69.4 us (0.82)
  Pallas kernels: 79.6 us -> 64 us
    pallas_call x1, Pallas kernels: 79.6 us -> 64 us  [on_device(): pl.pallas_call(functools.partial(kernel, tiles, lifts, nb), out_shape=jax...]
where the time goes in v2:
time: 69.4 us; the launch traced here: 69.2 us
  Pallas kernels  64 us (92%)
  local copies, waits for them, and re-layouts  4.6 us (7%)
    pallas_call x1, Pallas kernels, on_device(): pl.pallas_call(functools.partial(kernel, tiles, lifts, nb), out_shape=jax...  64 us
    unnamed x1, local copies, waits for them, and re-layouts  4.6 us

profile of v2, /device:TPU:0, one launch (start us, length us, event | category | flops | bytes accessed | tf_op | source)
XLA Modules:
  0.0 69.2 jit_solution(3327056097614167854)
XLA Ops:
  0.7 64.0 %shard_map.73 = f32[16,256,256]{2,1,0:T(8,128)} custom-call(s32[1,1,4]{2,1,0:T(1,128)} %sources_ref.1, f32[1]{0:T(128)S(6)} %copy.10.spacing_ref, f32[16,256,256]{2,1,0:T(8,128)} %bitcast.9, f32[16,256,256]{2,1,0:T(8,128)} %bitcast.10, s32[256,256]{1,0:T(8,128)} %bitcast.13, f32[4,256,256]{2,1,0:T(8,128)} %bitcast.11, f32[4,256,256]{2,1,0:T(8,128)} %bitcast.12), custom_call_target="tpu_custom_call" | custom-call | flops 1000000000 | bytes 16777216 | tf_op jit(solution)/shard_map/pallas_call | solution.py:488
  64.6 4.6 %copy.11 = f32[1,16,1,256,256]{4,3,2,1,0:T(8,128)} copy(f32[1,16,1,256,256]{4,3,2,1,0:T(8,128)} %bitcast.8) | data formatting | bytes 8388608

commit v3 on v2

--- a/solution.py
+++ b/solution.py
@@ -407,50 +407,53 @@
     f_load.wait()
     halo_send(f0, ALL, 0, depth)
     reduce_cores(0)
-    spread_enter(0)
     prepare_up()
     v_load.wait()
     i_load.wait()
     halo_receive(ALL)
     top_part(f0, f1, ALL)
-    for stage in range(nb):
+    for stage in range(nb - 1):
         reduce_next(0, stage)
+    spread_enter(0)
+    bottom_part(f0, f1, ALL)
+    reduce_next(0, nb - 1)
+    inner(f0, f1, ALL, 1, 4)
+    for stage in range(nb - 1):
         spread_next(0, stage)
-        if stage == 0:
-            bottom_part(f0, f1, ALL)
-            inner(f0, f1, ALL, 1, 3)
-    inner(f0, f1, ALL, 3, 7)
 
     for c in chunks:
         top_add(0, f1, c)
         if_above(top_up, 1, c, "start")
-        inner(f0, f1, ALL, 7 + 2 * c, 9 + 2 * c)
+        inner(f0, f1, ALL, 4 + c, 5 + c)
+    spread_next(0, nb - 1)
+    inner(f0, f1, ALL, 8, depth - 1)
+    halo_send(f1, INNER, 1, depth - 1)
+    halo_send(f1, TOP, depth - 1, depth)
     spread_next(0, nb)
+    spread_enter(1)
     project_up(0)
     bottom_add(0, f1)
-    spread_enter(1)
+    spread_next(1, 0)
     project_down(f1[0])
     reduce_enter(1)
-    halo_send(f1, INNER, 1, depth - 1)
-    halo_send(f1, TOP, depth - 1, depth)
+    for stage in range(1, nb):
+        spread_next(1, stage)
     halo_send(f1, BOTTOM, 0, 1)
     reduce_cores(1)
-    spread_next(1, 0)
     halo_receive(INNER)
-    inner(f1, f2, INNER, 1, 3)
-    for stage in range(nb):
+    inner(f1, f2, INNER, 1, 4)
+    for stage in range(nb - 1):
         reduce_next(1, stage)
-        spread_next(1, stage + 1)
-        if stage == 0:
-            halo_receive(BOTTOM)
-            bottom_part(f1, f2, BOTTOM)
-            halo_receive(TOP)
-            top_part(f1, f2, TOP)
-            inner(f1, f2, INNER, 3, 6)
+    spread_next(1, nb)
     project_up(1)
+    reduce_next(1, nb - 1)
+    halo_receive(BOTTOM)
+    bottom_part(f1, f2, BOTTOM)
     bottom_add(1, f2)
-    inner(f1, f2, INNER, 6, 8)
+    inner(f1, f2, INNER, 4, 8)
     put(0, 8, 0).start()
+    halo_receive(TOP)
+    top_part(f1, f2, TOP)
     inner(f1, f2, INNER, 8, depth - 1)
     put(8, depth - 9, 1).start()
     for c in chunks:
@@ -472,6 +475,18 @@
     put(0, 8, 0).wait()
     put(8, depth - 9, 1).wait()
     put(depth - 1, 1, 2).wait()
+
+
+def hand_over(parts, source, target, sems):
+    count = source.shape[0] // parts
+    copies = [
+        pltpu.make_async_copy(source.at[pl.ds(i * count, count)], target.at[pl.ds(i * count, count)], sems.at[i])
+        for i in range(parts)
+    ]
+    for copy in copies:
+        copy.start()
+    for copy in copies:
+        copy.wait()
 
 
 def on_device(tiles, lifts, oxygen, velocity, spacing, inlets, proj_x, proj_y, sources):
@@ -534,6 +549,14 @@
         ),
         cost_estimate=pl.CostEstimate(flops=10**9, bytes_accessed=16 * 1024 * 1024, transcendentals=0),
     )(sources, spacing, field, speed, inlets[0, 0], proj_x[0, 0], proj_y[0, 0])
+    parts = depth // 2
+    result = pl.pallas_call(
+        functools.partial(hand_over, parts),
+        out_shape=jax.ShapeDtypeStruct(field.shape, F32),
+        in_specs=[any_spec],
+        out_specs=any_spec,
+        scratch_shapes=[dma((parts,))],
+    )(result)
     return result[None, :, None]
 
 

time: 69.4 us -> 190 us (2.74)
  Pallas kernels: 64 us -> 189 us
  local copies, waits for them, and re-layouts: 4.6 us -> 0 us
    pallas_call x0 -> x1, Pallas kernels: none -> 128 us  [on_device(): pl.pallas_call(functools.partial(hand_over, parts), out_shape=jax.ShapeDt...]
    unnamed x1 -> x0, local copies, waits for them, and re-layouts: 4.6 us -> none
    pallas_call x1, Pallas kernels: 64 us -> 60.9 us  [on_device(): pl.pallas_call(functools.partial(kernel, tiles, lifts, nb), out_shape=jax...]
where the time goes in v3:
time: 190 us
  Pallas kernels  189 us (99%)
    pallas_call x1, Pallas kernels, on_device(): pl.pallas_call(functools.partial(hand_over, parts), out_shape=jax.ShapeDt...  128 us
    pallas_call x1, Pallas kernels, on_device(): pl.pallas_call(functools.partial(kernel, tiles, lifts, nb), out_shape=jax...  60.9 us

profile of v3, /device:TPU:0, one launch (start us, length us, event | category | flops | bytes accessed | tf_op | source)
XLA Modules:
  0.0 189.8 jit_solution(9587217642390775038)
XLA Ops:
  0.7 60.9 %shard_map.73.source = f32[16,256,256]{2,1,0:T(8,128)} custom-call(s32[1,1,4]{2,1,0:T(1,128)} %sources_ref.1, f32[1]{0:T(128)S(6)} %copy.9.spacing_ref, f32[16,256,256]{2,1,0:T(8,128)} %bitcast.8, f32[16,256,256]{2,1,0:T(8,128)} %bitcast.9, s32[256,256]{1,0:T(8,128)} %bitcast.12, f32[4,256,256]{2,1,0:T(8,128)} %bitcast.10, f32[4,256,256]{2,1,0:T(8,128)} %bitcast.11), custom_call_target="tpu_custom_call" | custom-call | flops 1000000000 | bytes 16777216 | tf_op jit(solution)/shard_map/pallas_call | solution.py:503
  61.6 128.2 %shard_map.74 = f32[16,256,256]{2,1,0:T(8,128)} custom-call(f32[16,256,256]{2,1,0:T(8,128)} %shard_map.73.source), custom_call_target="tpu_custom_call" | custom-call | tf_op jit(solution)/shard_map/pallas_call | solution.py:553

commit v4 on v3

--- a/solution.py
+++ b/solution.py
@@ -475,18 +475,6 @@
     put(0, 8, 0).wait()
     put(8, depth - 9, 1).wait()
     put(depth - 1, 1, 2).wait()
-
-
-def hand_over(parts, source, target, sems):
-    count = source.shape[0] // parts
-    copies = [
-        pltpu.make_async_copy(source.at[pl.ds(i * count, count)], target.at[pl.ds(i * count, count)], sems.at[i])
-        for i in range(parts)
-    ]
-    for copy in copies:
-        copy.start()
-    for copy in copies:
-        copy.wait()
 
 
 def on_device(tiles, lifts, oxygen, velocity, spacing, inlets, proj_x, proj_y, sources):
@@ -549,14 +537,6 @@
         ),
         cost_estimate=pl.CostEstimate(flops=10**9, bytes_accessed=16 * 1024 * 1024, transcendentals=0),
     )(sources, spacing, field, speed, inlets[0, 0], proj_x[0, 0], proj_y[0, 0])
-    parts = depth // 2
-    result = pl.pallas_call(
-        functools.partial(hand_over, parts),
-        out_shape=jax.ShapeDtypeStruct(field.shape, F32),
-        in_specs=[any_spec],
-        out_specs=any_spec,
-        scratch_shapes=[dma((parts,))],
-    )(result)
     return result[None, :, None]
 
 

time: 190 us -> 66.3 us (0.35)
  Pallas kernels: 189 us -> 60.9 us
  local copies, waits for them, and re-layouts: 0 us -> 4.6 us
    pallas_call x1 -> x0, Pallas kernels: 128 us -> none  [on_device(): pl.pallas_call(functools.partial(hand_over, parts), out_shape=jax.ShapeDt...]
    unnamed x0 -> x1, local copies, waits for them, and re-layouts: none -> 4.6 us
where the time goes in v4:
time: 66.3 us; the launch traced here: 66.2 us
  Pallas kernels  60.9 us (92%)
  local copies, waits for them, and re-layouts  4.6 us (7%)
    pallas_call x1, Pallas kernels, on_device(): pl.pallas_call(functools.partial(kernel, tiles, lifts, nb), out_shape=jax...  60.9 us
    unnamed x1, local copies, waits for them, and re-layouts  4.6 us

profile of v4, /device:TPU:0, one launch (start us, length us, event | category | flops | bytes accessed | tf_op | source)
XLA Modules:
  0.0 66.2 jit_solution(18433783754968365925)
XLA Ops:
  0.7 60.9 %shard_map.73 = f32[16,256,256]{2,1,0:T(8,128)} custom-call(s32[1,1,4]{2,1,0:T(1,128)} %sources_ref.1, f32[1]{0:T(128)S(6)} %copy.10.spacing_ref, f32[16,256,256]{2,1,0:T(8,128)} %bitcast.9, f32[16,256,256]{2,1,0:T(8,128)} %bitcast.10, s32[256,256]{1,0:T(8,128)} %bitcast.13, f32[4,256,256]{2,1,0:T(8,128)} %bitcast.11, f32[4,256,256]{2,1,0:T(8,128)} %bitcast.12), custom_call_target="tpu_custom_call" | custom-call | flops 1000000000 | bytes 16777216 | tf_op jit(solution)/shard_map/pallas_call | solution.py:491
  61.6 4.6 %copy.11 = f32[1,16,1,256,256]{4,3,2,1,0:T(8,128)} copy(f32[1,16,1,256,256]{4,3,2,1,0:T(8,128)} %bitcast.8) | data formatting | bytes 8388608
